TPU v7x, 512 devices: a whole 4x8x8 slice. The times are simulated.
512 devices in a mesh: group: 16 (over y, core), sub: 32 (over z, x).
Axes of the slice: x: 4, y: 8, z: 8, core: 2. Of those that a mesh axis runs over, the one named last changes fastest.
Arguments:
- right_side: float32 [262144, 128], P(('group', 'sub')), may hold values from -6 to 6
- mass: float32 [512, 512], P(('group', 'sub')), may hold values from 0.05 to 0.5
- block_values: float32 [262144, 512], P(('group', 'sub')), may hold values from 0.000390625 to 0.005859375
- block_cols: int32 [4096, 8], P(('group', 'sub')), may hold values from 0 to 7, as said below
- face_rows: int32 [512, 256], P(('group', 'sub')), may hold values from 0 to 511, as said below
- land_rows: int32 [512, 256], P(('group', 'sub')), may hold values from 0 to 511, as said below
- face_counts: int32 [512, 32], P(('group', 'sub')), may hold values from 0 to 8, as said below
- face_weight: float32 [512, 256], P(('group', 'sub')), may hold values from 0.3 to 3
- local_factor: float32 [262144, 128], P(('group', 'sub')), may hold values from -0.25 to 0.25
- basis: float32 [32768, 512], P(('group', 'sub')), may hold values from -0.25 to 0.25
- coarse_inverse: float32 [2048, 2048], P('sub'), may hold values from -1 to 2.5, as said below
Outputs:
- solution_field: float32 [262144, 128], P(('group', 'sub'))
- residual: float32 [262144, 128], P(('group', 'sub'))
Inputs may be any that keep to these rules, and one draw needn't show every extreme that they name: `block_cols`: for each k, the column blocks of a subdomain's 8 block rows are a permutation of 0 to 7. `face_rows`: the 256 entries of a subdomain are distinct local rows. `land_rows`: the 256 entries of a subdomain are distinct local rows. `face_counts`: every subdomain has 8 live slots toward at least one peer. `coarse_inverse`: symmetric positive definite.
All inputs are finite; a program needn't handle non-finite values.
Results may differ from a plain program's by a relative error of at most 0.0003.
Values sent between devices are 32-bit elements; how exact they have to be, the bound alone decides.
No kernel may reach another device: no remote copies, remote signals or barrier semaphores. Data moves between devices by JAX's collectives and lax.ppermute only.
A program may use at most 64 MiB of HBM per device.

v0:
```python
import jax
import jax.numpy as jnp
from jax import lax
from jax.sharding import PartitionSpec as P

ITERS = 3
highest = lax.Precision.HIGHEST


def local(
    right_side,
    mass,
    block_values,
    block_cols,
    face_rows,
    land_rows,
    face_counts,
    face_weight,
    local_factor,
    basis,
    coarse_inverse,
):
    n_rows, n_rhs = right_side.shape
    n_peers = lax.axis_size("sub")
    n_slots = face_rows.shape[1]
    per_peer = n_slots // n_peers
    n_blocks, n_stored = block_cols.shape
    block_rows = n_rows // n_blocks
    n_coarse = basis.shape[0]
    factor_rows = local_factor.shape[1]
    faces = face_rows[0]
    lands = land_rows[0]
    slot_ids = jnp.arange(n_slots)
    live = slot_ids % per_peer < face_counts[0][slot_ids // per_peer]
    weights = jnp.where(live, face_weight[0], jnp.float32(0.0))
    received = lax.all_to_all(weights, "sub", split_axis=0, concat_axis=0, tiled=True)
    values_r = block_values.reshape(n_blocks, block_rows, n_stored * block_rows)
    flat_cols = block_cols.reshape(-1)
    row_total = jnp.sum(block_values, axis=1)
    col_part = jnp.sum(values_r, axis=1).reshape(n_blocks * n_stored, block_rows)
    col_total = (
        jnp.zeros((n_blocks, block_rows), jnp.float32).at[flat_cols].add(col_part).reshape(n_rows)
    )
    degree = (row_total + col_total).at[faces].add(weights).at[lands].add(received)
    diag_col = (mass[0] + degree)[:, None]
    factor_r = local_factor.reshape(n_rows // factor_rows, factor_rows, factor_rows)

    def precondition(resid):
        jacobi = resid / diag_col
        blocks = resid.reshape(n_rows // factor_rows, factor_rows, n_rhs)
        inner = jnp.einsum("bij,bjc->bic", factor_r, blocks, precision=highest)
        local_part = jnp.einsum("bji,bjc->bic", factor_r, inner, precision=highest).reshape(
            n_rows, n_rhs
        )
        coarse_part = jnp.dot(basis, resid, precision=highest)
        total_coarse = coarse_inverse.shape[1]
        start = lax.axis_index("sub") * n_coarse
        padded = lax.dynamic_update_slice_in_dim(
            jnp.zeros((total_coarse, n_rhs), jnp.float32), coarse_part, start, 0
        )
        whole = lax.psum(padded, ("group", "sub"))
        solved = jnp.dot(coarse_inverse, whole, precision=highest)
        coarse_term = jnp.einsum("nr,nc->rc", basis, solved, precision=highest)
        return jacobi + local_part + coarse_term

    def residual_product(resid, zvalue):
        return lax.psum(jnp.sum(resid * zvalue, axis=0), ("group", "sub"))

    resid = right_side
    solution = jnp.zeros_like(right_side)
    zvalue = precondition(resid)
    direction = zvalue
    gamma = residual_product(resid, zvalue)
    for iteration in range(ITERS):
        got_out = lax.all_to_all(
            weights[:, None] * direction[faces], "sub", split_axis=0, concat_axis=0, tiled=True
        )
        got_back = lax.all_to_all(direction[lands], "sub", split_axis=0, concat_axis=0, tiled=True)
        operate_blocks = direction.reshape(n_blocks, block_rows, n_rhs)
        picked = operate_blocks[block_cols].reshape(n_blocks, n_stored * block_rows, n_rhs)
        forward = jnp.einsum("rik,rkc->ric", values_r, picked, precision=highest).reshape(
            n_rows, n_rhs
        )
        back_terms = jnp.einsum(
            "rik,ric->rkc", values_r, operate_blocks, precision=highest
        ).reshape(n_blocks * n_stored, block_rows, n_rhs)
        backward = (
            jnp.zeros((n_blocks, block_rows, n_rhs), jnp.float32)
            .at[flat_cols]
            .add(back_terms)
            .reshape(n_rows, n_rhs)
        )
        coupled = jnp.zeros((n_rows, n_rhs), jnp.float32).at[lands].add(got_out)
        coupled = coupled.at[faces].add(weights[:, None] * got_back)
        image = diag_col * direction - forward - backward - coupled
        alpha = gamma / lax.psum(jnp.sum(direction * image, axis=0), ("group", "sub"))
        solution = solution + alpha * direction
        resid = resid - alpha * image
        if iteration + 1 < ITERS:
            zvalue = precondition(resid)
            gamma_new = residual_product(resid, zvalue)
            direction = zvalue + gamma_new / gamma * direction
            gamma = gamma_new
    return (solution, resid)


def solution(mesh):
    placed = (
        P(("group", "sub"), None),
        P(("group", "sub"), None),
        P(("group", "sub"), None),
        P(("group", "sub"), None),
        P(("group", "sub"), None),
        P(("group", "sub"), None),
        P(("group", "sub"), None),
        P(("group", "sub"), None),
        P(("group", "sub"), None),
        P(("group", "sub"), None),
        P("sub", None),
    )
    return jax.shard_map(
        local,
        mesh=mesh,
        in_specs=placed,
        out_specs=(P(("group", "sub"), None), P(("group", "sub"), None)),
        check_vma=False,
    )
```

profile of v0, /device:TPU:1, one launch (start us, length us, event | category | flops | bytes accessed | tf_op | source)
XLA Modules:
  0.0 1505.4 jit_solution(3155422974275814790)
XLA Ops:
  11.5 5.2 compare_select_fusion.3
  16.7 16.3 %compare_select_fusion.11 = (f32[256]{0:T(256)S(1)}, s32[256]{0:T(256)S(1)}) fusion(f32[256]{0:T(256)} %bitcast.231, pred[256]{0:T(512)(128)(4,1)S(1)} %get-tuple-element.59, pred[256]{0:T(512)(128)(4,1)S(1)} %get-tuple-element.60, pred[256]{0:T(512)(128)(4,1)S(1)} %get-tuple-element.61, pred[256]{0:T(512)(128)(4,1)S(1)} %get-tuple-element.62, ...), kind=kLoop, calls=%fused_computation.136 | loop fusion | flops 8448 | bytes 10596 | tf_op jit(solution)/shard_map/jit(_where)/select_n | solution.py:35
  35.7 13.7 all-to-all-start
  61.1 268.2 %all-reduce.5.cloned.1.call-done = f32[2048,128]{1,0:T(8,128)} async-done(((f32[2048,128]{1,0:T(8,128)}), f32[2048,128]{1,0:T(8,128)}) %all-reduce.5.cloned.1.call-update) | async-done | bytes 1048592 | tf_op jit(solution)/shard_map/psum | solution.py:61
  333.5 6.8 all-to-all-start.1
  340.3 3.2 convolution_bitcast_fusion.2
  346.4 7.0 scatter_fusion.2
  357.1 9.2 all-to-all-start.2
  371.3 4.4 all-to-all-done.2
  378.9 97.2 %all-reduce = (f32[128]{0:T(128)S(1)}, f32[128]{0:T(128)S(1)}) all-reduce(f32[128]{0:T(128)} %get-tuple-element.9, f32[128]{0:T(128)} %get-tuple-element.8), channel_id=1, replica_groups=mesh['group'=16,'sub'=32] {'group','sub'}, use_global_device_ids=true, to_apply=%region_7.8 | all-reduce | flops 256 | bytes 2048 | tf_op jit(solution)/shard_map/psum | solution.py:67
  479.7 265.3 %all-reduce.7.cloned.1.call-done = f32[2048,128]{1,0:T(8,128)} async-done(((f32[2048,128]{1,0:T(8,128)}), f32[2048,128]{1,0:T(8,128)}) %all-reduce.7.cloned.1.call-update) | async-done | bytes 1048592 | tf_op jit(solution)/shard_map/psum | solution.py:61
  747.6 97.2 %psum.67 = f32[128]{0:T(128)S(1)} all-reduce(f32[128]{0:T(128)S(1)} %get-tuple-element.53), channel_id=1, replica_groups=mesh['group'=16,'sub'=32] {'group','sub'}, use_global_device_ids=true, to_apply=%region_15.16 | all-reduce | flops 128 | bytes 1024 | tf_op jit(solution)/shard_map/psum | solution.py:67
  850.0 5.9 all-to-all-start.3
  862.0 7.0 scatter_fusion.3
  869.2 9.5 all-to-all-start.4
  883.9 4.1 all-to-all-done.4
  891.3 95.4 %psum.68 = f32[128]{0:T(128)S(1)} all-reduce(f32[128]{0:T(128)} %get-tuple-element.14), channel_id=1, replica_groups=mesh['group'=16,'sub'=32] {'group','sub'}, use_global_device_ids=true, to_apply=%region_20.21 | all-reduce | flops 128 | bytes 1024 | tf_op jit(solution)/shard_map/psum | solution.py:96
  990.9 265.1 %all-reduce.9.cloned.1.call-done = f32[2048,128]{1,0:T(8,128)} async-done(((f32[2048,128]{1,0:T(8,128)}), f32[2048,128]{1,0:T(8,128)}) %all-reduce.9.cloned.1.call-update) | async-done | bytes 1048592 | tf_op jit(solution)/shard_map/psum | solution.py:61
  1258.6 97.4 %psum.70 = f32[128]{0:T(128)S(1)} all-reduce(f32[128]{0:T(128)S(1)} %get-tuple-element.55), channel_id=1, replica_groups=mesh['group'=16,'sub'=32] {'group','sub'}, use_global_device_ids=true, to_apply=%region_23.24 | all-reduce | flops 128 | bytes 1024 | tf_op jit(solution)/shard_map/psum | solution.py:67
  1361.2 5.7 all-to-all-start.5
  1373.0 7.0 scatter_fusion.4
  1380.2 9.2 all-to-all-start.6
  1394.4 4.4 all-to-all-done.6
  1401.4 95.4 %psum.71 = f32[128]{0:T(128)S(1)} all-reduce(f32[128]{0:T(128)S(1)} %get-tuple-element.12), channel_id=1, replica_groups=mesh['group'=16,'sub'=32] {'group','sub'}, use_global_device_ids=true, to_apply=%region_28.29 | all-reduce | flops 128 | bytes 1024 | tf_op jit(solution)/shard_map/psum | solution.py:96
  (191 shorter events, 90.6 us)
Async XLA Ops:
  7.2 322.2 %copy-start = (f32[64,2048]{1,0:T(8,128)S(1)}, f32[64,2048]{1,0:T(8,128)}, u32[]{:S(2)}) copy-start(f32[64,2048]{1,0:T(8,128)} %param.21) | copy-start | bytes 1572868
  7.2 45.0 %copy-start.17 = (f32[1,256]{1,0:T(1,128)S(1)}, f32[1,256]{1,0:T(1,128)}, u32[]{:S(2)}) copy-start(f32[1,256]{1,0:T(1,128)} %param.18) | copy-start | bytes 3076
  7.2 44.8 %copy-start.14 = (s32[8,8]{1,0:T(8,128)S(1)}, s32[8,8]{1,0:T(8,128)}, u32[]{:S(2)}) copy-start(s32[8,8]{1,0:T(8,128)} %param.14) | copy-start | bytes 772
  7.2 45.0 %copy-start.1 = (f32[512,512]{1,0:T(8,128)S(1)}, f32[512,512]{1,0:T(8,128)}, u32[]{:S(2)}) copy-start(f32[512,512]{1,0:T(8,128)} %param.13) | copy-start | bytes 3145732
  16.7 39.0 %copy-start.16 = (s32[256,1]{0,1:T(1,128)}, s32[256,1]{0,1:T(1,128)S(1)}, u32[]{:S(2)}) copy-start(s32[256,1]{0,1:T(1,128)S(1)} %get-tuple-element.57) | copy-start | bytes 3076
  35.7 22.3 %all-to-all-start = ((f32[32,8,1]{1,2,0:T(1,128)}), f32[32,8,1]{1,2,0:T(1,128)S(1)}, u32[]{:S(2)}, u32[]{:S(2)}) async-start(f32[32,8,1]{1,2,0:T(1,128)} %bitcast.41), calls=%async_computation | async-start | bytes 32768 | tf_op jit(solution)/shard_map/all_to_all | solution.py:36
  49.4 280.0 %all-reduce.5.cloned.1.call-start = ((), (), s32[]{:S(2)}) async-start(), calls=%async_computation.7 | async-start | bytes 2097152 | tf_op jit(solution)/shard_map/psum | solution.py:61
  52.3 294.1 %copy-start.18 = (s32[64]{0:T(128)}, s32[64]{0:T(128)S(1)}, u32[]{:S(2)}) copy-start(s32[64]{0:T(128)S(1)} %fusion.36) | copy-start | bytes 772
  54.1 278.6 %copy-start.11 = (f32[32,8]{1,0:T(8,128)}, f32[32,8]{1,0:T(8,128)S(1)}, u32[]{:S(2)}) copy-start(f32[32,8]{1,0:T(8,128)S(1)} %fusion.32) | copy-start | bytes 3076
  58.0 273.4 %copy-start.9 = (f32[64,512]{1,0:T(8,128)S(1)}, f32[64,512]{1,0:T(8,128)}, u32[]{:S(2)}) copy-start(f32[64,512]{1,0:T(8,128)} %param.20) | copy-start | bytes 393220
  331.8 512.9 %copy-start.6 = (f32[512,128]{0,1:T(8,128)}, f32[512,128]{0,1:T(8,128)S(1)}, u32[]{:S(2)}) copy-start(f32[512,128]{0,1:T(8,128)S(1)} %fusion.2) | copy-start | bytes 786436
  333.5 23.6 %all-to-all-start.1 = ((f32[32,8,128]{2,1,0:T(8,128)}), f32[32,8,128]{2,1,0:T(8,128)S(1)}, u32[]{:S(2)}, u32[]{:S(2)}) async-start(f32[32,8,128]{2,1,0:T(8,128)} %bitcast_multiply_fusion.8), calls=%async_computation.1 | async-start | bytes 262144 | tf_op jit(solution)/shard_map/all_to_all | solution.py:75
  357.1 18.6 %all-to-all-start.2 = ((f32[32,8,128]{2,1,0:T(8,128)}), f32[32,8,128]{2,1,0:T(8,128)S(1)}, u32[]{:S(2)}, u32[]{:S(2)}) async-start(f32[32,8,128]{2,1,0:T(8,128)} %bitcast.56), calls=%async_computation.2 | async-start | bytes 262144 | tf_op jit(solution)/shard_map/all_to_all | solution.py:78
  366.3 378.7 %all-reduce.7.cloned.1.call-start = ((), (), s32[]{:S(2)}) async-start(), calls=%async_computation.8 | async-start | bytes 2097152 | tf_op jit(solution)/shard_map/psum | solution.py:61
  479.0 365.8 %copy-start.30 = (f32[128]{0:T(128)S(1)}, f32[128]{0:T(128)}, u32[]{:S(2)}) copy-start(f32[128]{0:T(128)} %copy-done.29) | copy-start | bytes 1540
  850.0 19.2 %all-to-all-start.3 = ((f32[32,8,128]{2,1,0:T(8,128)}), f32[32,8,128]{2,1,0:T(8,128)S(1)}, u32[]{:S(2)}, u32[]{:S(2)}) async-start(f32[32,8,128]{2,1,0:T(8,128)} %bitcast_multiply_fusion.5), calls=%async_computation.3 | async-start | bytes 262144 | tf_op jit(solution)/shard_map/all_to_all | solution.py:75
  869.2 18.8 %all-to-all-start.4 = ((f32[32,8,128]{2,1,0:T(8,128)}), f32[32,8,128]{2,1,0:T(8,128)}, u32[]{:S(2)}, u32[]{:S(2)}) async-start(f32[32,8,128]{2,1,0:T(8,128)} %bitcast.71), calls=%async_computation.4 | async-start | bytes 262144 | tf_op jit(solution)/shard_map/all_to_all | solution.py:78
  878.7 377.4 %all-reduce.9.cloned.1.call-start = ((), (), s32[]{:S(2)}) async-start(), calls=%async_computation.9 | async-start | bytes 2097152 | tf_op jit(solution)/shard_map/psum | solution.py:61
  990.2 365.8 %copy-start.28 = (f32[128]{0:T(128)S(1)}, f32[128]{0:T(128)}, u32[]{:S(2)}) copy-start(f32[128]{0:T(128)} %copy-done.27) | copy-start | bytes 1540
  1361.2 19.0 %all-to-all-start.5 = ((f32[32,8,128]{2,1,0:T(8,128)}), f32[32,8,128]{2,1,0:T(8,128)S(1)}, u32[]{:S(2)}, u32[]{:S(2)}) async-start(f32[32,8,128]{2,1,0:T(8,128)} %bitcast_multiply_fusion.2), calls=%async_computation.5 | async-start | bytes 262144 | tf_op jit(solution)/shard_map/all_to_all | solution.py:75
  1380.2 18.6 %all-to-all-start.6 = ((f32[32,8,128]{2,1,0:T(8,128)}), f32[32,8,128]{2,1,0:T(8,128)S(1)}, u32[]{:S(2)}, u32[]{:S(2)}) async-start(f32[32,8,128]{2,1,0:T(8,128)} %bitcast.86), calls=%async_computation.6 | async-start | bytes 262144 | tf_op jit(solution)/shard_map/all_to_all | solution.py:78
  1392.6 104.2 %copy-start.7 = (f32[512,128]{0,1:T(8,128)S(1)}, f32[512,128]{0,1:T(8,128)}, u32[]{:S(2)}) copy-start(f32[512,128]{0,1:T(8,128)} %copy-done.6) | copy-start | bytes 786436
  1392.6 104.2 %copy-start.23 = (f32[128]{0:T(128)S(1)}, f32[128]{0:T(128)}, u32[]{:S(2)}) copy-start(f32[128]{0:T(128)} %copy-done.22) | copy-start | bytes 1540
  1392.7 104.2 %copy-start.25 = (f32[128]{0:T(128)S(1)}, f32[128]{0:T(128)}, u32[]{:S(2)}) copy-start(f32[128]{0:T(128)} %copy-done.24) | copy-start | bytes 1540
  (17 other events, 49.6 us)
Sparse Core Ops, SparseCore 0:
  55.3 274.0 all-reduce.4
  478.4 266.6 all-reduce.6
  989.7 266.3 all-reduce.8
where the time goes:
time: 1520 us; the launch traced here: 1510 us
  waiting for transfers between devices  812 us (53%)
  blocking collectives  483 us (32%)
  other arithmetic  69.2 us (5%)
  starting transfers between devices  60.2 us (4%)
  local copies, waits for them, and re-layouts  34.9 us (2%)
  matrix products  32.1 us (2%)
    psum x3, waiting for transfers between devices, precondition(): whole = lax.psum(padded, ('group', 'sub'))  799 us
    psum x3, blocking collectives, residual_product(): return lax.psum(jnp.sum(resid * zvalue, axis=0), ('group', 'sub'))  292 us
    psum x2, blocking collectives, local(): lax.psum(jnp.sum(direction * image, axis=0), ('group', 'sub'))  191 us
  transfers between devices with their start and end apart: 10, of which 6 were waited for; matrix products, arithmetic and copies ran while one was open for 5% of the time, Pallas kernels for 0%

commit v1 on v0

--- a/solution.py
+++ b/solution.py
@@ -64,7 +64,7 @@
         return jacobi + local_part + coarse_term
 
     def residual_product(resid, zvalue):
-        return lax.psum(jnp.sum(resid * zvalue, axis=0), ("group", "sub"))
+        return lax.psum(lax.psum(jnp.sum(resid * zvalue, axis=0), "sub"), "group")
 
     resid = right_side
     solution = jnp.zeros_like(right_side)

time: 1520 us -> 1610 us (1.059)
  blocking collectives: 483 us -> 572 us
    psum x2 -> x3, blocking collectives: 191 us -> 284 us  [local(): lax.psum(jnp.sum(direction * image, axis=0), ('group', 'sub'))]
    psum x3 -> x6, blocking collectives: 292 us -> 288 us  [residual_product(): return lax.psum(lax.psum(jnp.sum(resid * zvalue, axis=0), 'sub'), 'group')]
  transfers between devices with their start and end apart: 10 -> 10, of which waited for: 6 -> 6; matrix products, arithmetic and copies ran while one was open for 5% -> 4% of each run, Pallas kernels for 0% -> 0%
where the time goes in v1:
time: 1610 us; the launch traced here: 1600 us
  waiting for transfers between devices  813 us (50%)
  blocking collectives  572 us (36%)
  other arithmetic  69.2 us (4%)
  starting transfers between devices  63.1 us (4%)
  local copies, waits for them, and re-layouts  34.9 us (2%)
  matrix products  32.1 us (2%)
    psum x3, waiting for transfers between devices, precondition(): whole = lax.psum(padded, ('group', 'sub'))  800 us
    psum x6, blocking collectives, residual_product(): return lax.psum(lax.psum(jnp.sum(resid * zvalue, axis=0), 'sub'), 'group')  288 us
    psum x3, blocking collectives, local(): lax.psum(jnp.sum(direction * image, axis=0), ('group', 'sub'))  284 us
  transfers between devices with their start and end apart: 10, of which 6 were waited for; matrix products, arithmetic and copies ran while one was open for 4% of the time, Pallas kernels for 0%

profile of v1, /device:TPU:1, one launch (start us, length us, event | category | flops | bytes accessed | tf_op | source)
XLA Modules:
  0.0 1599.3 jit_solution(906750239872124390)
XLA Ops:
  11.5 5.2 compare_select_fusion.3
  16.7 16.3 %compare_select_fusion.11 = (f32[256]{0:T(256)S(1)}, s32[256]{0:T(256)S(1)}) fusion(f32[256]{0:T(256)} %bitcast.231, pred[256]{0:T(512)(128)(4,1)S(1)} %get-tuple-element.57, pred[256]{0:T(512)(128)(4,1)S(1)} %get-tuple-element.58, pred[256]{0:T(512)(128)(4,1)S(1)} %get-tuple-element.59, pred[256]{0:T(512)(128)(4,1)S(1)} %get-tuple-element.60, ...), kind=kLoop, calls=%fused_computation.136 | loop fusion | flops 8448 | bytes 10596 | tf_op jit(solution)/shard_map/jit(_where)/select_n | solution.py:35
  35.7 13.7 all-to-all-start
  61.1 268.2 %all-reduce.4.cloned.1.call-done = f32[2048,128]{1,0:T(8,128)} async-done(((f32[2048,128]{1,0:T(8,128)}), f32[2048,128]{1,0:T(8,128)}) %all-reduce.4.cloned.1.call-update) | async-done | bytes 1048592 | tf_op jit(solution)/shard_map/psum | solution.py:61
  333.5 6.8 all-to-all-start.1
  346.4 7.0 scatter_fusion.2
  357.1 9.2 all-to-all-start.2
  378.9 56.8 %psum.85 = f32[128]{0:T(128)S(1)} all-reduce(f32[128]{0:T(128)} %get-tuple-element.9), channel_id=1, replica_groups=mesh['group'=16,'sub'=32] {'sub'}, use_global_device_ids=true, to_apply=%region_7.8 | all-reduce | flops 128 | bytes 1024 | tf_op jit(solution)/shard_map/psum | solution.py:67
  435.7 40.3 %psum.86 = f32[128]{0:T(128)S(1)} all-reduce(f32[128]{0:T(128)S(1)} %psum.85), channel_id=1, replica_groups=mesh['group'=16,'sub'=32] {'group'}, use_global_device_ids=true, to_apply=%region_8.9 | all-reduce | flops 128 | bytes 1024 | tf_op jit(solution)/shard_map/psum | solution.py:67
  476.0 93.6 %psum.87 = f32[128]{0:T(128)S(1)} all-reduce(f32[128]{0:T(128)} %get-tuple-element.8), channel_id=1, replica_groups=mesh['group'=16,'sub'=32] {'group','sub'}, use_global_device_ids=true, to_apply=%region_13.14 | all-reduce | flops 128 | bytes 1024 | tf_op jit(solution)/shard_map/psum | solution.py:96
  573.2 266.1 %all-reduce.6.cloned.1.call-done = f32[2048,128]{1,0:T(8,128)} async-done(((f32[2048,128]{1,0:T(8,128)}), f32[2048,128]{1,0:T(8,128)}) %all-reduce.6.cloned.1.call-update) | async-done | bytes 1048592 | tf_op jit(solution)/shard_map/psum | solution.py:61
  841.8 58.4 %psum.89 = f32[128]{0:T(128)S(1)} all-reduce(f32[128]{0:T(128)S(1)} %get-tuple-element.51), channel_id=1, replica_groups=mesh['group'=16,'sub'=32] {'sub'}, use_global_device_ids=true, to_apply=%region_16.17 | all-reduce | flops 128 | bytes 1024 | tf_op jit(solution)/shard_map/psum | solution.py:67
  900.2 37.0 %psum.90 = f32[128]{0:T(128)S(1)} all-reduce(f32[128]{0:T(128)S(1)} %psum.89), channel_id=1, replica_groups=mesh['group'=16,'sub'=32] {'group'}, use_global_device_ids=true, to_apply=%region_17.18 | all-reduce | flops 128 | bytes 1024 | tf_op jit(solution)/shard_map/psum | solution.py:67
  942.5 7.4 all-to-all-start.3
  955.9 7.0 scatter_fusion.3
  963.1 9.5 all-to-all-start.4
  985.2 95.1 %psum.91 = f32[128]{0:T(128)S(1)} all-reduce(f32[128]{0:T(128)} %get-tuple-element.12), channel_id=1, replica_groups=mesh['group'=16,'sub'=32] {'group','sub'}, use_global_device_ids=true, to_apply=%region_22.23 | all-reduce | flops 128 | bytes 1024 | tf_op jit(solution)/shard_map/psum | solution.py:96
  1084.6 266.1 %all-reduce.8.cloned.1.call-done = f32[2048,128]{1,0:T(8,128)} async-done(((f32[2048,128]{1,0:T(8,128)}), f32[2048,128]{1,0:T(8,128)}) %all-reduce.8.cloned.1.call-update) | async-done | bytes 1048592 | tf_op jit(solution)/shard_map/psum | solution.py:61
  1353.2 58.4 %psum.93 = f32[128]{0:T(128)S(1)} all-reduce(f32[128]{0:T(128)S(1)} %get-tuple-element.53), channel_id=1, replica_groups=mesh['group'=16,'sub'=32] {'sub'}, use_global_device_ids=true, to_apply=%region_25.26 | all-reduce | flops 128 | bytes 1024 | tf_op jit(solution)/shard_map/psum | solution.py:67
  1411.7 37.0 %psum.94 = f32[128]{0:T(128)S(1)} all-reduce(f32[128]{0:T(128)S(1)} %psum.93), channel_id=1, replica_groups=mesh['group'=16,'sub'=32] {'group'}, use_global_device_ids=true, to_apply=%region_26.27 | all-reduce | flops 128 | bytes 1024 | tf_op jit(solution)/shard_map/psum | solution.py:67
  1453.9 7.2 all-to-all-start.5
  1467.2 7.0 scatter_fusion.4
  1474.4 9.2 all-to-all-start.6
  1495.5 95.1 %psum.95 = f32[128]{0:T(128)S(1)} all-reduce(f32[128]{0:T(128)S(1)} %get-tuple-element.10), channel_id=1, replica_groups=mesh['group'=16,'sub'=32] {'group','sub'}, use_global_device_ids=true, to_apply=%region_31.32 | all-reduce | flops 128 | bytes 1024 | tf_op jit(solution)/shard_map/psum | solution.py:96
  (195 shorter events, 106.7 us)
Async XLA Ops:
  7.2 322.2 %copy-start = (f32[64,2048]{1,0:T(8,128)S(1)}, f32[64,2048]{1,0:T(8,128)}, u32[]{:S(2)}) copy-start(f32[64,2048]{1,0:T(8,128)} %param.21) | copy-start | bytes 1572868
  7.2 45.0 %copy-start.17 = (f32[1,256]{1,0:T(1,128)S(1)}, f32[1,256]{1,0:T(1,128)}, u32[]{:S(2)}) copy-start(f32[1,256]{1,0:T(1,128)} %param.18) | copy-start | bytes 3076
  7.2 44.8 %copy-start.14 = (s32[8,8]{1,0:T(8,128)S(1)}, s32[8,8]{1,0:T(8,128)}, u32[]{:S(2)}) copy-start(s32[8,8]{1,0:T(8,128)} %param.14) | copy-start | bytes 772
  7.2 45.0 %copy-start.1 = (f32[512,512]{1,0:T(8,128)S(1)}, f32[512,512]{1,0:T(8,128)}, u32[]{:S(2)}) copy-start(f32[512,512]{1,0:T(8,128)} %param.13) | copy-start | bytes 3145732
  35.7 22.3 %all-to-all-start = ((f32[32,8,1]{1,2,0:T(1,128)}), f32[32,8,1]{1,2,0:T(1,128)S(1)}, u32[]{:S(2)}, u32[]{:S(2)}) async-start(f32[32,8,1]{1,2,0:T(1,128)} %bitcast.41), calls=%async_computation | async-start | bytes 32768 | tf_op jit(solution)/shard_map/all_to_all | solution.py:36
  49.4 280.0 %all-reduce.4.cloned.1.call-start = ((), (), s32[]{:S(2)}) async-start(), calls=%async_computation.7 | async-start | bytes 2097152 | tf_op jit(solution)/shard_map/psum | solution.py:61
  52.3 294.1 %copy-start.18 = (s32[64]{0:T(128)}, s32[64]{0:T(128)S(1)}, u32[]{:S(2)}) copy-start(s32[64]{0:T(128)S(1)} %fusion.36) | copy-start | bytes 772
  54.1 278.6 %copy-start.11 = (f32[32,8]{1,0:T(8,128)}, f32[32,8]{1,0:T(8,128)S(1)}, u32[]{:S(2)}) copy-start(f32[32,8]{1,0:T(8,128)S(1)} %fusion.32) | copy-start | bytes 3076
  58.0 273.4 %copy-start.9 = (f32[64,512]{1,0:T(8,128)S(1)}, f32[64,512]{1,0:T(8,128)}, u32[]{:S(2)}) copy-start(f32[64,512]{1,0:T(8,128)} %param.20) | copy-start | bytes 393220
  331.8 605.4 %copy-start.6 = (f32[512,128]{0,1:T(8,128)}, f32[512,128]{0,1:T(8,128)S(1)}, u32[]{:S(2)}) copy-start(f32[512,128]{0,1:T(8,128)S(1)} %fusion.2) | copy-start | bytes 786436
  333.5 23.6 %all-to-all-start.1 = ((f32[32,8,128]{2,1,0:T(8,128)}), f32[32,8,128]{2,1,0:T(8,128)S(1)}, u32[]{:S(2)}, u32[]{:S(2)}) async-start(f32[32,8,128]{2,1,0:T(8,128)} %bitcast_multiply_fusion.8), calls=%async_computation.1 | async-start | bytes 262144 | tf_op jit(solution)/shard_map/all_to_all | solution.py:75
  357.1 18.6 %all-to-all-start.2 = ((f32[32,8,128]{2,1,0:T(8,128)}), f32[32,8,128]{2,1,0:T(8,128)S(1)}, u32[]{:S(2)}, u32[]{:S(2)}) async-start(f32[32,8,128]{2,1,0:T(8,128)} %bitcast.56), calls=%async_computation.2 | async-start | bytes 262144 | tf_op jit(solution)/shard_map/all_to_all | solution.py:78
  366.3 473.0 %all-reduce.6.cloned.1.call-start = ((), (), s32[]{:S(2)}) async-start(), calls=%async_computation.8 | async-start | bytes 2097152 | tf_op jit(solution)/shard_map/psum | solution.py:61
  476.0 93.6 %copy-start.29 = (f32[128]{0:T(128)}, f32[128]{0:T(128)S(1)}, u32[]{:S(2)}) copy-start(f32[128]{0:T(128)S(1)} %psum.86) | copy-start | bytes 1540
  572.4 364.8 %copy-start.30 = (f32[128]{0:T(128)S(1)}, f32[128]{0:T(128)}, u32[]{:S(2)}) copy-start(f32[128]{0:T(128)} %copy-done.29) | copy-start | bytes 1540
  942.5 20.7 %all-to-all-start.3 = ((f32[32,8,128]{2,1,0:T(8,128)}), f32[32,8,128]{2,1,0:T(8,128)S(1)}, u32[]{:S(2)}, u32[]{:S(2)}) async-start(f32[32,8,128]{2,1,0:T(8,128)} %bitcast_multiply_fusion.5), calls=%async_computation.3 | async-start | bytes 262144 | tf_op jit(solution)/shard_map/all_to_all | solution.py:75
  963.1 18.8 %all-to-all-start.4 = ((f32[32,8,128]{2,1,0:T(8,128)}), f32[32,8,128]{2,1,0:T(8,128)}, u32[]{:S(2)}, u32[]{:S(2)}) async-start(f32[32,8,128]{2,1,0:T(8,128)} %bitcast.71), calls=%async_computation.4 | async-start | bytes 262144 | tf_op jit(solution)/shard_map/all_to_all | solution.py:78
  972.6 378.1 %all-reduce.8.cloned.1.call-start = ((), (), s32[]{:S(2)}) async-start(), calls=%async_computation.9 | async-start | bytes 2097152 | tf_op jit(solution)/shard_map/psum | solution.py:61
  1083.9 364.8 %copy-start.28 = (f32[128]{0:T(128)S(1)}, f32[128]{0:T(128)}, u32[]{:S(2)}) copy-start(f32[128]{0:T(128)} %copy-done.27) | copy-start | bytes 1540
  1453.9 20.5 %all-to-all-start.5 = ((f32[32,8,128]{2,1,0:T(8,128)}), f32[32,8,128]{2,1,0:T(8,128)S(1)}, u32[]{:S(2)}, u32[]{:S(2)}) async-start(f32[32,8,128]{2,1,0:T(8,128)} %bitcast_multiply_fusion.2), calls=%async_computation.5 | async-start | bytes 262144 | tf_op jit(solution)/shard_map/all_to_all | solution.py:75
  1474.4 18.6 %all-to-all-start.6 = ((f32[32,8,128]{2,1,0:T(8,128)}), f32[32,8,128]{2,1,0:T(8,128)S(1)}, u32[]{:S(2)}, u32[]{:S(2)}) async-start(f32[32,8,128]{2,1,0:T(8,128)} %bitcast.86), calls=%async_computation.6 | async-start | bytes 262144 | tf_op jit(solution)/shard_map/all_to_all | solution.py:78
  1486.8 103.9 %copy-start.7 = (f32[512,128]{0,1:T(8,128)S(1)}, f32[512,128]{0,1:T(8,128)}, u32[]{:S(2)}) copy-start(f32[512,128]{0,1:T(8,128)} %copy-done.6) | copy-start | bytes 786436
  1486.8 103.9 %copy-start.23 = (f32[128]{0:T(128)S(1)}, f32[128]{0:T(128)}, u32[]{:S(2)}) copy-start(f32[128]{0:T(128)} %copy-done.22) | copy-start | bytes 1540
  1486.8 103.9 %copy-start.25 = (f32[128]{0:T(128)S(1)}, f32[128]{0:T(128)}, u32[]{:S(2)}) copy-start(f32[128]{0:T(128)} %copy-done.24) | copy-start | bytes 1540
  (17 other events, 88.1 us)
Sparse Core Ops, SparseCore 0:
  55.3 274.0 all-reduce.3
  571.9 267.3 all-reduce.5
  1083.3 267.3 all-reduce.7
